TPU v7x, 512 devices: a whole 4x4x16 slice. The times are simulated.
512 devices in a mesh: dp: 64 (over y, z), tensor: 8 (over x, core).
Axes of the slice: x: 4, y: 4, z: 16, core: 2. Of those that a mesh axis runs over, the one named last changes fastest.
Arguments:
- context: bfloat16 [6144, 4096], P('dp', 'tensor'), may hold values from -0.25 to 0.25
- residual: bfloat16 [6144, 8192], P('tensor', 'dp'), may hold values from -300 to 300
- gain: float32 [8192], P('dp'), may hold values from 0.25 to 1.75
- start: float32 [4096, 8192], P('tensor', 'dp'), may hold values from -12 to 12
Outputs:
- basis: float32 [3, 4096, 8192], P(None, 'tensor', 'dp')
- alphas: float32 [2], replicated
- betas: float32 [2], replicated
All inputs are finite; a program needn't handle non-finite values.
Results may differ from a plain program's by a relative error of at most 0.025.
Values may be sent and summed in bfloat16 or wider, within the bound.
A program may use at most 64 MiB of HBM per device.

v0:
```python
import functools

import jax
import jax.numpy as jnp
from jax import lax
from jax.experimental import pallas as pl
from jax.experimental.pallas import tpu as pltpu
from jax.sharding import PartitionSpec as P

ITERS = 2
SCALE = 2.0 ** -20
NX = 4
LB = 128
F32, BF16 = jnp.float32, jnp.bfloat16


def lanczos_coefs(g, total):
    g = [[g[i][j] / total for j in range(3)] for i in range(3)]

    def inner(a, b):
        return sum(a[i] * b[j] * g[i][j] for i in range(3) for j in range(3))

    def axpy(a, b, s):
        return [b[i] - s * a[i] for i in range(3)]

    zero = jnp.zeros_like(g[0][0])
    inv = 1.0 / jnp.sqrt(g[0][0] + 1e-06)
    q0 = [inv, zero, zero]
    w1 = [zero, inv / SCALE, zero]
    h00 = inner(q0, w1)
    r1 = axpy(q0, w1, h00)
    b0 = jnp.sqrt(jnp.maximum(inner(r1, r1), 0.0) + 1e-06)
    q1 = [v / b0 for v in r1]
    gw1 = [zero, zero, inv / SCALE / SCALE]
    w2 = [v / b0 for v in axpy(w1, gw1, h00)]
    h01 = inner(q0, w2)
    h11 = inner(q1, w2)
    r2 = axpy(q1, axpy(q0, w2, h01), h11)
    b1 = jnp.sqrt(jnp.maximum(inner(r2, r2), 0.0) + 1e-06)
    q2 = [v / b1 for v in r2]
    return (q0, q1, q2), (h00, h11), (b0, b1)


def kernel(cfg, ctx, res, gain, start, basis, ab, C, R, ST, GN, VT, UT, CT, TS, ER, WS, XR, TB, RR, W, P1, P2, GC, GX, GZ, send, recv, local):
    NZ, RU, FB, DB, D, CTX = cfg
    NT = NZ * 3 * RU
    RB = 3 * RU
    HALF = NZ // 2
    nrow = NT // LB
    i = lax.axis_index("dp")
    t = lax.axis_index("tensor")
    y, z = i // NZ, i % NZ
    x, c = t // 2, t % 2
    o = 1 - c

    def dev(dx=0, dy=0, dz=0, core=None):
        return {
            "dp": ((y + dy) % NX) * NZ + (z + dz) % NZ,
            "tensor": ((x + dx) % NX) * 2 + (c if core is None else core),
        }

    def turned(core):
        return {"dp": x * NZ + z, "tensor": y * 2 + core}

    partner = dev(core=o)
    xs = [dev(dx=k) for k in (1, 2, 3)]
    ys = [dev(dy=k) for k in (1, 2, 3)]
    right, left = dev(dz=1), dev(dz=NZ - 1)

    count = [0]
    pending = []

    def xfer(src, dst, to):
        n = count[0]
        count[0] += 1
        return pltpu.make_async_remote_copy(
            src_ref=src, dst_ref=dst, send_sem=send.at[n], recv_sem=recv.at[n],
            device_id=to, device_id_type=pl.DeviceIdType.MESH,
        )

    def go(src, dst, to):
        copy = xfer(src, dst, to)
        copy.start()
        pending.append(copy)
        return copy

    def drain(keep):
        for copy in pending[:len(pending) - keep]:
            copy.wait_send()
        del pending[:len(pending) - keep]

    def signal(to):
        pl.semaphore_signal(barrier, 1, device_id=to, device_id_type=pl.DeviceIdType.MESH)

    barrier = pltpu.get_barrier_semaphore()
    near = [partner] + xs + ys + [right, left]
    for p in near:
        signal(p)

    @pl.when(x != y)
    def _():
        signal(turned(0))
        signal(turned(1))

    own_rows = pl.ds(pl.multiple_of(z * RB, RU), RB)
    fcol = pl.ds(pl.multiple_of(y * FB, FB), FB)
    mine = pl.ds(pl.multiple_of(x * FB, FB), FB)
    half = [pl.ds(pl.multiple_of(k * RB, RU), RB) for k in (c, o)]
    getst = pltpu.make_async_copy(start, ST, local.at[2])
    getst.start()
    getgn = pltpu.make_async_copy(gain, GN, local.at[3])
    getgn.start()
    rmine = pltpu.make_async_copy(res.at[:, half[0]], R.at[pl.ds(c * HALF, HALF)], local.at[1])
    rmine.start()
    keep = pltpu.make_async_copy(ctx.at[half[0]], C.at[c, own_rows, mine], local.at[0])

    @pl.when(x == y)
    def _():
        keep.start()

    getst.wait()
    st = ST[...].T
    W[0] = st
    VT[0, c, :, mine] = st.astype(BF16)

    @pl.when(x != y)
    def _():
        pl.semaphore_wait(barrier, len(near) + 2)

    @pl.when(x == y)
    def _():
        pl.semaphore_wait(barrier, len(near))

    same = xfer(ctx.at[half[0]], C.at[c, own_rows, mine], turned(c))

    @pl.when(x != y)
    def _():
        same.start()

    other = go(ctx.at[half[1]], C.at[c, own_rows, mine], turned(o))

    def gather_vector(slot):
        out = [go(VT.at[slot, c, :, mine], VT.at[slot, c, :, mine], p) for p in xs]
        back = [go(VT.at[slot, c, :, mine], VT.at[slot, c, :, mine], partner)]
        return out, back

    def forward_vector(slot, out, back):
        for k in (1, 3, 2):
            out[k - 1].wait_recv()
            blk = pl.ds(pl.multiple_of(((x + NX - k) % NX) * FB, FB), FB)
            back.append(go(VT.at[slot, c, :, blk], VT.at[slot, c, :, blk], partner))

    vout, vback = gather_vector(0)
    rswap = go(res.at[:, half[1]], R.at[pl.ds(c * HALF, HALF)], partner)

    @pl.when(x != y)
    def _():
        same.wait()

    @pl.when(x == y)
    def _():
        keep.wait()

    other.wait_recv()

    def third(zz):
        return pl.ds(pl.multiple_of(zz * RB, RU), RU)

    def rest(zz):
        return pl.ds(pl.multiple_of(zz * RB + RU, RU), 2 * RU)

    def rest_of(zz, h):
        return pl.ds(pl.multiple_of(zz * RB + RU + h * RU, RU), RU)

    def send_third(h, zz, to):
        return go(C.at[h, third(zz)], C.at[h, third(zz)], to)

    def send_rest(zz, to):
        return go(C.at[:, rest(zz), fcol], C.at[:, rest(zz), fcol], to)

    def send_rest_half(h, zz, to):
        return go(C.at[h, rest(zz), fcol], C.at[h, rest(zz), fcol], to)

    def ycopies(zz):
        return zz, send_rest(zz, ys[0]), send_rest(zz, ys[2])

    last = []

    def yforward(item):
        zz, up, down = item
        below = pl.ds(pl.multiple_of(((y + NX - 1) % NX) * FB, FB), FB)
        above = pl.ds(pl.multiple_of(((y + 1) % NX) * FB, FB), FB)
        up.wait_recv()
        last.append(go(C.at[:, rest_of(zz, 0), below], C.at[:, rest_of(zz, 0), below], ys[0]))
        down.wait_recv()
        last.append(go(C.at[:, rest_of(zz, 1), above], C.at[:, rest_of(zz, 1), above], ys[2]))

    first = [dev(dy=a, dz=b) for b in (1, 0) for a in (2, 1, 3, 0) if a or b]
    second = [dev(dz=(HALF + k) % NZ) for k in sorted(range(0, NZ, 2), key=lambda v: min(v, NZ - v)) if (HALF + k) % NZ]

    def fan(buf, call, peers):
        return [go(buf.at[call, 0], buf.at[call, k + 1], p) for k, p in enumerate(peers)]

    def add_up(buf, call, copies):
        total = buf[call, 0]
        for k, copy in reversed(list(enumerate(copies))):
            copy.wait_recv()
            total = total + buf[call, k + 1]
        return total

    def fan_first(call, a1, a2):
        for j in range(nrow):
            P1[call, 0, j:j + 1, :] = a1[:, j * LB:(j + 1) * LB]
            P1[call, 0, nrow + j:nrow + j + 1, :] = a2[:, j * LB:(j + 1) * LB]
        return fan(P1, call, first)

    def fan_second(call, copies):
        P2[call, 0] = add_up(P1, call, copies)
        return fan(P2, call, second)

    def finish(call, copies):
        v = add_up(P2, call, copies)
        return (jnp.concatenate([v[j:j + 1] for j in range(nrow)], axis=1),
                jnp.concatenate([v[nrow + j:nrow + j + 1] for j in range(nrow)], axis=1))

    ar, al = [None, None], [None, None]
    for h in (0, 1):
        ar[h], al[h] = send_rest_half(h, z, right), send_rest_half(h, z, left)
    y1 = [go(C.at[:, third(z), fcol], C.at[:, third(z), fcol], p) for p in ys]
    queue = [[], [ycopies(z)]]
    for copy in y1:
        copy.wait_recv()
    br, bl = [None, None], [None, None]
    for h in (0, 1):
        br[h], bl[h] = send_third(h, z, right), send_third(h, z, left)

    getgn.wait()
    gsq = GN[...] * GN[...]
    g2 = jnp.broadcast_to(gsq, (DB, DB)).T[:, 0:1]

    for s in range(1, HALF + 1):
        zr, zl = (z + NZ - s) % NZ, (z + s) % NZ
        end = s == HALF
        for h in (0, 1):
            if not end or h == 0:
                ar[h].wait_recv()
            if s < HALF - 1 or (not end and h == 0):
                ar[h] = send_rest_half(h, zr, right)
            if not end or h == 1:
                al[h].wait_recv()
            if s < HALF - 1 or (not end and h == 1):
                al[h] = send_rest_half(h, zl, left)
        now = [ycopies(zr)] if end else [ycopies(zr), ycopies(zl)]
        if end:
            sums0 = fan_second(0, sums0)
        for h in (0, 1):
            if not end or h == 0:
                br[h].wait_recv()
            if s < HALF - 1 or (not end and h == 0):
                br[h] = send_third(h, zr, right)
            if not end or h == 1:
                bl[h].wait_recv()
            if s < HALF - 1 or (not end and h == 1):
                bl[h] = send_third(h, zl, left)
        queue.append(now)
        for item in queue.pop(0):
            yforward(item)
        if s == 3:
            forward_vector(0, vout, vback)
        if s == 2:
            rmine.wait()
            rswap.wait_recv()
            rt = R[...].reshape(NT, DB).astype(F32).T
            UT[...] = rt
            sq = rt * rt
            sums0 = fan_first(0, jnp.sum(sq, axis=0, keepdims=True), jnp.sum(sq * g2, axis=0, keepdims=True))
    for items in queue:
        for item in items:
            yforward(item)
    for copy in vback + last:
        copy.wait_recv()

    MB = NT // 2
    pairs = [(a, b) for b in range(3) for a in range(b + 1)]
    zeros = jnp.zeros((8, LB), F32)

    def gram_rows(b):
        for n, (p, q) in enumerate(pairs):
            if q == b:
                prod = jnp.sum(W[p] * W[q], axis=0, keepdims=True)
                GC[0, n:n + 1, :] = functools.reduce(
                    lambda m, v: m + v, [prod[:, j * LB:(j + 1) * LB] for j in range(FB // LB)])

    GC[0] = zeros
    for step in range(ITERS):
        def rows(m, carry, step=step):
            r = pl.ds(pl.multiple_of(m * MB, LB), MB)
            acc = lax.dot_general(C[0, r, :], VT[step, 0], (((1,), (1,)), ((), ())), preferred_element_type=F32)
            acc += lax.dot_general(C[1, r, :], VT[step, 1], (((1,), (1,)), ((), ())), preferred_element_type=F32)
            CT[:, r] = acc.T
            return carry

        lax.fori_loop(0, 2, rows, 0)
        uc = UT[...] * CT[...]
        sums = fan_first(1 + step, jnp.sum(uc, axis=0, keepdims=True), jnp.sum(uc * g2, axis=0, keepdims=True))
        drain(len(sums))
        if step == 0:
            s1, s2 = finish(0, sums0)
            ms = s1 / D + 1e-06
            TS[0:1, :] = 1.0 / ms
            TS[1:2, :] = 1.0 / jnp.sqrt(ms)
            TS[2:3, :] = s2 / ms
        sums = fan_second(1 + step, sums)
        gram_rows(step)
        a1, a2 = finish(1 + step, sums)
        ims, irms = TS[0:1, :], TS[1:2, :]
        along = a1 * irms / D
        back = a2 * irms / D - along * (TS[2:3, :] / D)
        ER[...] = ((g2 * (CT[...] - UT[...] * (irms * along)) - UT[...] * (irms * back)) * ims).astype(BF16)

        swaps, outs = {}, {}

        def swap(k):
            col = pl.ds(pl.multiple_of(((x + k) % NX) * FB, FB), FB)
            WS[step, :, col] = jnp.dot(ER[...], C[o, :, col], preferred_element_type=F32).astype(BF16)
            swaps[k] = go(WS.at[step, :, col], XR.at[step, :, col], partner)
            TB[k] = jnp.dot(ER[...], C[c, :, col], preferred_element_type=F32)

        def out(k):
            col = pl.ds(pl.multiple_of(((x + k) % NX) * FB, FB), FB)
            swaps[k].wait_recv()
            total = TB[k] + XR[step, :, col].astype(F32)
            if k:
                RR[step, 3 + k] = total.astype(BF16)
                outs[k] = go(RR.at[step, 3 + k], RR.at[step, k], xs[k - 1])
            return total

        order = (2, 1, 3, 0)
        swap(order[0])
        for n in (1, 2, 3):
            swap(order[n])
            out(order[n - 1])
        total = out(0)
        for k in (1, 3, 2):
            outs[k].wait_recv()
            total = total + RR[step, k].astype(F32)
        total = total * SCALE
        W[step + 1] = total
        if step + 1 < ITERS:
            VT[step + 1, c, :, mine] = total.astype(BF16)
            vout, vback = gather_vector(step + 1)
            forward_vector(step + 1, vout, vback)
            for copy in vback:
                copy.wait_recv()

    gram_rows(2)
    copy = go(GC.at[0], GC.at[1], partner)
    copy.wait_recv()
    xy = x * NX + y
    GX[xy] = GC[0] + GC[1]
    copies = [go(GX.at[xy], GX.at[xy], dev(dx=a, dy=b)) for a in (2, 1, 3, 0) for b in (2, 1, 3, 0) if a or b]
    for copy in copies:
        copy.wait_recv()
    v = functools.reduce(lambda m, w: m + w, [GX[k] for k in range(NX * NX)])
    v = jnp.sum(v, axis=1, keepdims=True)
    lane = lax.broadcasted_iota(jnp.int32, (8, LB), 1)
    GZ[z] = jnp.sum(jnp.where(lane == lax.broadcasted_iota(jnp.int32, (8, LB), 0), v, 0.0), axis=0, keepdims=True)
    far = sorted(range(1, NZ), key=lambda k: -min(k, NZ - k))
    copies = [go(GZ.at[z], GZ.at[z], dev(dz=k)) for k in far]
    drain(len(far))
    for copy in copies:
        copy.wait_recv()
    v = functools.reduce(lambda m, w: m + w, [GZ[k] for k in range(NZ)])
    g = [[None] * 3 for _ in range(3)]
    for n, (a, b) in enumerate(pairs):
        g[a][b] = g[b][a] = jnp.sum(jnp.where(lane[0:1] == n, v, 0.0), axis=1, keepdims=True)
    qs, alphas, betas = lanczos_coefs(g, float(CTX * D))
    for n, q in enumerate(qs):
        basis[n] = sum(q[k] * W[k] for k in range(n + 1)).T
    for n, value in enumerate(alphas + betas):
        ab[n:n + 1, :] = jnp.broadcast_to(value, (1, LB))
    ab[4:8, :] = jnp.zeros((4, LB), F32)
    drain(0)


def body(cfg, context, residual, gain, start):
    NZ, RU, FB, DB, D, CTX = cfg
    NT, RB = NZ * 3 * RU, 3 * RU
    vmem = pl.BlockSpec(memory_space=pltpu.VMEM)
    flops = 8 * NT * CTX * DB
    basis, ab = pl.pallas_call(
        functools.partial(kernel, cfg),
        out_shape=(jax.ShapeDtypeStruct((3, FB, DB), F32), jax.ShapeDtypeStruct((8, LB), F32)),
        in_specs=[pl.BlockSpec(memory_space=pltpu.HBM)] * 4,
        out_specs=(vmem, vmem),
        scratch_shapes=[
            pltpu.VMEM((2, NT, NX * FB), BF16),
            pltpu.VMEM((NZ, RB, DB), BF16),
            pltpu.VMEM((FB, DB), F32),
            pltpu.VMEM((1, DB), F32),
            pltpu.VMEM((ITERS, 2, DB, NX * FB), BF16),
            pltpu.VMEM((DB, NT), F32),
            pltpu.VMEM((DB, NT), F32),
            pltpu.VMEM((8, NT), F32),
            pltpu.VMEM((DB, NT), BF16),
            pltpu.VMEM((ITERS, DB, NX * FB), BF16),
            pltpu.VMEM((ITERS, DB, NX * FB), BF16),
            pltpu.VMEM((4, DB, FB), F32),
            pltpu.VMEM((ITERS, 7, DB, FB), BF16),
            pltpu.VMEM((3, DB, FB), F32),
            pltpu.VMEM((ITERS + 1, 8, 2 * (NT // LB), LB), F32),
            pltpu.VMEM((ITERS + 1, NZ // 2, 2 * (NT // LB), LB), F32),
            pltpu.VMEM((2, 8, LB), F32),
            pltpu.VMEM((NX * NX, 8, LB), F32),
            pltpu.VMEM((NZ, 1, LB), F32),
            pltpu.SemaphoreType.DMA((320,)),
            pltpu.SemaphoreType.DMA((320,)),
            pltpu.SemaphoreType.DMA((4,)),
        ],
        compiler_params=pltpu.CompilerParams(collective_id=0, has_side_effects=True, vmem_limit_bytes=40 * 2 ** 20),
        cost_estimate=pl.CostEstimate(flops=flops, bytes_accessed=2 ** 21, transcendentals=0),
    )(context, residual.reshape(NZ // 2, 2 * RB, DB), gain.reshape(1, DB), start)
    return basis, ab[0:2, 0], ab[2:4, 0]


def solution(mesh):
    cfg = (16, 16, 512, 128, 8192, 4096)
    in_specs = (P("dp", "tensor"), P("tensor", "dp"), P("dp"), P("tensor", "dp"))
    out_specs = (P(None, "tensor", "dp"), P(), P())
    return jax.shard_map(
        functools.partial(body, cfg), mesh=mesh, in_specs=in_specs, out_specs=out_specs, check_vma=False)
```

profile of v0, /device:TPU:1, one launch (start us, length us, event | category | flops | bytes accessed | tf_op | source)
XLA Modules:
  0.0 146.1 jit_solution(5252592794575882877)
XLA Ops:
  0.6 0.0 copy-start.3
  0.6 0.6 copy-done.3
  1.3 0.0 copy-start
  1.3 0.9 copy-done
  2.2 0.0 copy-start.1
  2.2 0.9 copy-done.1
  3.2 0.0 copy-start.2
  3.2 0.9 copy-done.2
  4.1 140.5 %shard_map.67 = (f32[3,512,128]{2,1,0:T(8,128)S(1)}, f32[8,128]{1,0:T(8,128)S(1)}) custom-call(bf16[96,512]{1,0:T(8,128)(2,1)S(1)} %copy-done.2, bf16[8,96,128]{2,1,0:T(8,128)(2,1)S(1)} %bitcast.2, f32[1,128]{1,0:T(1,128)S(1)} %bitcast.3, f32[512,128]{1,0:T(8,128)S(1)} %copy-done), custom_call_target="tpu_custom_call" | custom-call | flops 3221225472 | bytes 2097152 | tf_op jit(solution)/shard_map/pallas_call | solution.py:391
  144.6 0.7 slice_reduce_fusion
  145.2 0.9 copy.8
Async XLA Ops:
  0.6 0.7 copy-start.3
  1.3 0.9 copy-start
  2.2 0.9 copy-start.1
  3.2 0.9 copy-start.2
where the time goes:
time: 146 us
  Pallas kernels  141 us (97%)
  local copies, waits for them, and re-layouts  4.96 us (3%)
    pallas_call x1, Pallas kernels, body(): pl.pallas_call(functools.partial(kernel, cfg), out_shape=(jax.ShapeDtypeS...  141 us
    unnamed x9, local copies, waits for them, and re-layouts  4.3 us

commit v1 on v0

--- a/solution.py
+++ b/solution.py
@@ -354,14 +354,18 @@
                 copy.wait_recv()
 
     gram_rows(2)
-    copy = go(GC.at[0], GC.at[1], partner)
-    copy.wait_recv()
-    xy = x * NX + y
-    GX[xy] = GC[0] + GC[1]
-    copies = [go(GX.at[xy], GX.at[xy], dev(dx=a, dy=b)) for a in (2, 1, 3, 0) for b in (2, 1, 3, 0) if a or b]
+    me = (x * NX + y) * 2 + c
+    GX[me] = GC[0]
+    copies = [
+        go(GX.at[me], GX.at[me], dev(dx=a, dy=b, core=k))
+        for a in (2, 1, 3, 0) for b in (2, 1, 3, 0) for k in ((c, o) if a or b else (o,))
+    ]
     for copy in copies:
         copy.wait_recv()
-    v = functools.reduce(lambda m, w: m + w, [GX[k] for k in range(NX * NX)])
+    parts = [GX[k] for k in range(2 * NX * NX)]
+    while len(parts) > 1:
+        parts = [p + q for p, q in zip(parts[::2], parts[1::2])]
+    v = parts[0]
     v = jnp.sum(v, axis=1, keepdims=True)
     lane = lax.broadcasted_iota(jnp.int32, (8, LB), 1)
     GZ[z] = jnp.sum(jnp.where(lane == lax.broadcasted_iota(jnp.int32, (8, LB), 0), v, 0.0), axis=0, keepdims=True)
@@ -411,7 +415,7 @@
             pltpu.VMEM((ITERS + 1, 8, 2 * (NT // LB), LB), F32),
             pltpu.VMEM((ITERS + 1, NZ // 2, 2 * (NT // LB), LB), F32),
             pltpu.VMEM((2, 8, LB), F32),
-            pltpu.VMEM((NX * NX, 8, LB), F32),
+            pltpu.VMEM((2 * NX * NX, 8, LB), F32),
             pltpu.VMEM((NZ, 1, LB), F32),
             pltpu.SemaphoreType.DMA((320,)),
             pltpu.SemaphoreType.DMA((320,)),

time: 146 us -> 146 us (level)
  no operation moved by 1% of the time
where the time goes in v1:
time: 146 us
  Pallas kernels  141 us (97%)
  local copies, waits for them, and re-layouts  4.96 us (3%)
    pallas_call x1, Pallas kernels, body(): pl.pallas_call(functools.partial(kernel, cfg), out_shape=(jax.ShapeDtypeS...  141 us
    unnamed x9, local copies, waits for them, and re-layouts  4.3 us

profile of v1, /device:TPU:1, one launch (start us, length us, event | category | flops | bytes accessed | tf_op | source)
XLA Modules:
  0.0 146.2 jit_solution(6061182606829213063)
XLA Ops:
  0.6 0.0 copy-start.3
  0.6 0.6 copy-done.3
  1.3 0.0 copy-start
  1.3 0.9 copy-done
  2.2 0.0 copy-start.1
  2.2 0.9 copy-done.1
  3.2 0.0 copy-start.2
  3.2 0.9 copy-done.2
  4.1 140.6 %shard_map.67 = (f32[3,512,128]{2,1,0:T(8,128)S(1)}, f32[8,128]{1,0:T(8,128)S(1)}) custom-call(bf16[96,512]{1,0:T(8,128)(2,1)S(1)} %copy-done.2, bf16[8,96,128]{2,1,0:T(8,128)(2,1)S(1)} %bitcast.2, f32[1,128]{1,0:T(1,128)S(1)} %bitcast.3, f32[512,128]{1,0:T(8,128)S(1)} %copy-done), custom_call_target="tpu_custom_call" | custom-call | flops 3221225472 | bytes 2097152 | tf_op jit(solution)/shard_map/pallas_call | solution.py:395
  144.7 0.7 slice_reduce_fusion
  145.3 0.9 copy.8
Async XLA Ops:
  0.6 0.7 copy-start.3
  1.3 0.9 copy-start
  2.2 0.9 copy-start.1
  3.2 0.9 copy-start.2
